TPU v7x, 512 devices: a whole 4x4x16 slice. The times are simulated.
512 devices in a mesh: seq: 64 (over x, z_lo, core), kvh: 8 (over z_hi, y).
Axes of the slice: x: 4, y: 4, z: 16 (z_hi: 2, z_lo: 8; z = z_hi * 8 + z_lo), core: 2. Of those that a mesh axis runs over, the one named last changes fastest.
Arguments:
- queries: bfloat16 [16384, 12288], P('seq', 'kvh'), may hold values from -4 to 4
- keys: bfloat16 [16384, 1024], P('seq', 'kvh'), may hold values from -10 to 10
- values: bfloat16 [16384, 1024], P('seq', 'kvh'), may hold values from -6 to 6
- answer_lengths: int32 [16], replicated, may hold values from 512 to 3072, as said below
Outputs:
- attended: bfloat16 [16384, 12288], P(('seq', 'kvh'))
Inputs may be any that keep to these rules, and one draw needn't show every extreme that they name: `answer_lengths`: every length is a multiple of 256; the lengths sum to 16384; exactly one answer has the largest length 3072, every other one at most (11) * 256.
All inputs are finite; a program needn't handle non-finite values.
Results may differ from a plain program's by a relative error of at most 0.0035.
Values may be sent and summed in bfloat16 or wider, within the bound.
A program may use at most 64 MiB of HBM per device.

v0:
```python
import functools
import math

import jax
import jax.numpy as jnp
from jax import lax
from jax.experimental import pallas as pl
from jax.experimental.pallas import tpu as pltpu
from jax.sharding import PartitionSpec as P

HEAD = 128
SPAN = 12
MESH = pl.DeviceIdType.MESH
LOW = -1e30
EXP2_SCALE = math.log2(math.e) / math.sqrt(HEAD)


def kernel(n_seq, n_kvh, len_ref, q_hbm, k_hbm, v_hbm, out_hbm, qv, kv, s_scr, stage,
           local_sem, main_send, main_recv, aux_send, aux_recv, out_send, out_recv):
    tokens, width = qv.shape
    heads = width // HEAD
    rows = tokens // n_kvh
    half = n_kvh // 2
    me = lax.axis_index("seq")
    mine = lax.axis_index("kvh")
    core = lax.rem(me, 2)
    my_hi = mine // half
    my_lo = lax.rem(mine, half)

    def seq_at(step):
        return lax.rem(me + (step + n_seq), n_seq)

    def peer(i):
        cross = i < half
        hi = jnp.where(cross, 1 - my_hi, my_hi)
        lo = lax.rem(my_lo + jnp.where(cross, i, i - half + 1), half)
        return hi * half + lo

    local = [
        pltpu.make_async_copy(k_hbm, kv.at[0, 0], local_sem.at[0]),
        pltpu.make_async_copy(v_hbm, kv.at[0, 1], local_sem.at[1]),
        pltpu.make_async_copy(q_hbm, qv, local_sem.at[2]),
    ]
    for copy in local:
        copy.start()

    barrier = pltpu.get_barrier_semaphore()
    for step in (-2, -1, 1, 2):
        pl.semaphore_signal(barrier, inc=1, device_id={"seq": seq_at(step)}, device_id_type=MESH)
    for i in range(n_kvh - 1):
        pl.semaphore_signal(barrier, inc=1, device_id={"kvh": peer(i)}, device_id_type=MESH)

    base = me * tokens
    first = jnp.int32(0)
    start = jnp.int32(0)
    for a in range(len_ref.shape[0]):
        first = jnp.where(start <= base, start, first)
        start = start + len_ref[a]

    local[0].wait()
    local[1].wait()
    pl.semaphore_wait(barrier, 4 + n_kvh - 1)

    def main_copy(t, part):
        return pltpu.make_async_remote_copy(
            src_ref=kv.at[2 * t, part], dst_ref=kv.at[2 * t + 2, part],
            send_sem=main_send.at[t, part], recv_sem=main_recv.at[t, part],
            device_id={"seq": seq_at(2)}, device_id_type=MESH)

    def aux_copy(u, part, src, step):
        return pltpu.make_async_remote_copy(
            src_ref=kv.at[src, part], dst_ref=kv.at[2 * u + 1, part],
            send_sem=aux_send.at[u, part], recv_sem=aux_recv.at[u, part],
            device_id={"seq": seq_at(step)}, device_id_type=MESH)

    for t in range(SPAN // 2):
        for part in range(2):
            if t > 0:
                main_copy(t - 1, part).wait_recv()
            if t < SPAN // 2 - 1:
                main_copy(t, part).start()

            @pl.when(core == 0)
            def _():
                aux_copy(t, part, 2 * t, 1).start()

            if t > 0:
                @pl.when(core == 1)
                def _():
                    aux_copy(t - 1, part, 2 * t, -1).start()
            if t == SPAN // 2 - 1:
                @pl.when(core == 1)
                def _():
                    aux_copy(t, part, 2 * t, 1).start()

    for u in range(SPAN // 2):
        for part in range(2):
            aux_copy(u, part, 0, 1).wait_recv()
    local[2].wait()

    def attend(row0):
        q = jnp.concatenate(
            [qv[pl.ds(row0, rows), h * HEAD:(h + 1) * HEAD] for h in range(heads)], axis=0)
        peak = jnp.full((heads * rows, HEAD), LOW, jnp.float32)
        for b in range(SPAN):
            s = lax.dot_general(q, kv[b, 0], (((1,), (1,)), ((), ())),
                                preferred_element_type=jnp.float32)
            if b == 0:
                token = row0 + lax.rem(lax.broadcasted_iota(jnp.int32, s.shape, 0), rows)
                s = jnp.where(lax.broadcasted_iota(jnp.int32, s.shape, 1) <= token, s, LOW)
            s_scr[:, b * tokens:(b + 1) * tokens] = s
            best = s[:, :HEAD]
            for j in range(1, tokens // HEAD):
                best = jnp.maximum(best, s[:, j * HEAD:(j + 1) * HEAD])
            if b > 0:
                best = jnp.where(b * tokens <= base - first, best, LOW)
            peak = jnp.maximum(peak, best)
        peak = jnp.max(peak, axis=1, keepdims=True)
        total = jnp.zeros((heads * rows, HEAD), jnp.float32)
        acc = jnp.zeros((heads * rows, HEAD), jnp.float32)
        for b in range(SPAN):
            shift = peak if b == 0 else jnp.where(b * tokens <= base - first, peak, -LOW)
            p = jnp.exp2((s_scr[:, b * tokens:(b + 1) * tokens] - shift) * EXP2_SCALE)
            for j in range(tokens // HEAD):
                total = total + p[:, j * HEAD:(j + 1) * HEAD]
            acc = acc + jnp.dot(p.astype(jnp.bfloat16), kv[b, 1], preferred_element_type=jnp.float32)
        return (acc / jnp.sum(total, axis=1, keepdims=True)).astype(jnp.bfloat16)

    def out_copy(i):
        columns = pl.ds(pl.multiple_of(mine * width, width), width)
        return pltpu.make_async_remote_copy(
            src_ref=stage.at[i], dst_ref=out_hbm.at[:, columns],
            send_sem=out_send.at[i], recv_sem=out_recv.at[i],
            device_id={"kvh": peer(i)}, device_id_type=MESH)

    def self_copy():
        columns = pl.ds(pl.multiple_of(mine * width, width), width)
        return pltpu.make_async_copy(stage.at[n_kvh - 1], out_hbm.at[:, columns], local_sem.at[3])

    def one_chunk(i, carry):
        target = jnp.where(i == n_kvh - 1, mine, peer(i))
        done = attend(pl.multiple_of(target * rows, rows))
        for h in range(heads):
            stage[i, :, h * HEAD:(h + 1) * HEAD] = done[h * rows:(h + 1) * rows, :]

        @pl.when(i < n_kvh - 1)
        def _():
            out_copy(i).start()

        return carry

    lax.fori_loop(0, n_kvh, one_chunk, 0)
    self_copy().start()
    self_copy().wait()
    for i in range(n_kvh - 1):
        out_copy(i).wait()
    for t in range(SPAN // 2):
        for part in range(2):
            if t < SPAN // 2 - 1:
                main_copy(t, part).wait_send()
            aux_copy(t, part, 0, 1).wait_send()


def shards(queries, keys, values, answer_lengths):
    tokens, width = queries.shape
    n_seq, n_kvh = lax.axis_size("seq"), lax.axis_size("kvh")
    rows = tokens // n_kvh
    heads = width // HEAD
    dma = pltpu.SemaphoreType.DMA
    any_spec = pl.BlockSpec(memory_space=pl.ANY)
    return pl.pallas_call(
        functools.partial(kernel, n_seq, n_kvh),
        out_shape=jax.ShapeDtypeStruct((rows, n_kvh * width), jnp.bfloat16),
        in_specs=[pl.BlockSpec(memory_space=pltpu.SMEM), any_spec, any_spec, any_spec],
        out_specs=any_spec,
        scratch_shapes=[
            pltpu.VMEM((tokens, width), jnp.bfloat16),
            pltpu.VMEM((SPAN, 2, tokens, HEAD), jnp.bfloat16),
            pltpu.VMEM((heads * rows, SPAN * tokens), jnp.float32),
            pltpu.VMEM((n_kvh, rows, width), jnp.bfloat16),
            dma((4,)),
            dma((SPAN // 2, 2)),
            dma((SPAN // 2, 2)),
            dma((SPAN // 2, 2)),
            dma((SPAN // 2, 2)),
            dma((n_kvh,)),
            dma((n_kvh,)),
        ],
        compiler_params=pltpu.CompilerParams(
            collective_id=0, has_side_effects=True, vmem_limit_bytes=48 * 1024 * 1024),
        cost_estimate=pl.CostEstimate(
            flops=4 * tokens * width * SPAN * tokens,
            bytes_accessed=4 * tokens * width,
            transcendentals=tokens * heads * SPAN * tokens),
    )(answer_lengths, queries, keys, values)


def solution(mesh):
    in_specs = (P("seq", "kvh"), P("seq", "kvh"), P("seq", "kvh"), P())
    out_specs = P(("seq", "kvh"), None)
    return jax.shard_map(shards, mesh=mesh, in_specs=in_specs, out_specs=out_specs, check_vma=False)
```

profile of v0, /device:TPU:153, one launch (start us, length us, event | category | flops | bytes accessed | tf_op | source)
XLA Modules:
  0.0 86.2 jit_solution(3133327756054269602)
XLA Ops:
  0.0 0.0 copy-start
  0.0 1.1 %copy-done = bf16[256,1536]{1,0:T(8,128)(2,1)S(1)} copy-done((bf16[256,1536]{1,0:T(8,128)(2,1)S(1)}, bf16[256,1536]{1,0:T(8,128)(2,1)}, u32[]{:S(2)}) %copy-start) | copy-done | bytes 786456
  1.1 0.0 copy-start.1
  1.1 0.8 copy-done.1
  2.0 0.0 copy-start.2
  2.0 0.8 copy-done.2
  2.8 0.0 copy-start.3
  2.8 0.7 copy-done.3
  3.5 81.8 %shard_map.46 = bf16[32,12288]{1,0:T(8,128)(2,1)S(1)} custom-call(s32[16]{0:T(128)S(1)} %copy-done.3, bf16[256,1536]{1,0:T(8,128)(2,1)S(1)} %copy-done, bf16[256,128]{1,0:T(8,128)(2,1)S(1)} %copy-done.1, bf16[256,128]{1,0:T(8,128)(2,1)S(1)} %copy-done.2), custom_call_target="tpu_custom_call" | custom-call | flops 4831838208 | bytes 1572864 | tf_op jit(solution)/shard_map/pallas_call | solution.py:171
  85.3 0.9 %copy.6 = bf16[32,12288]{1,0:T(8,128)(2,1)} copy(bf16[32,12288]{1,0:T(8,128)(2,1)S(1)} %shard_map.46) | data formatting | bytes 1572864
Async XLA Ops:
  0.0 1.1 %copy-start = (bf16[256,1536]{1,0:T(8,128)(2,1)S(1)}, bf16[256,1536]{1,0:T(8,128)(2,1)}, u32[]{:S(2)}) copy-start(bf16[256,1536]{1,0:T(8,128)(2,1)} %q_hbm.1) | copy-start | bytes 2359300
  1.1 0.8 copy-start.1
  2.0 0.8 copy-start.2
  2.8 0.7 copy-start.3
where the time goes:
time: 86.5 us; the launch traced here: 86.2 us
  Pallas kernels  81.8 us (95%)
  local copies, waits for them, and re-layouts  4.35 us (5%)
    pallas_call x1, Pallas kernels, shards(): pl.pallas_call(functools.partial(kernel, n_seq, n_kvh), out_shape=jax.Sha...  81.8 us
    unnamed x9, local copies, waits for them, and re-layouts  4.35 us

commit v1 on v0

v1 whole, which is shorter than its diff:
```python
import functools
import math

import jax
import jax.numpy as jnp
from jax import lax
from jax.experimental import pallas as pl
from jax.experimental.pallas import tpu as pltpu
from jax.sharding import PartitionSpec as P

HEAD = 128
SPAN = 12
PARTS = 4
RUN = 8
MESH = pl.DeviceIdType.MESH
LOW = -1e30
EXP2_SCALE = math.log2(math.e) / math.sqrt(HEAD)


def kernel(n_seq, n_kvh, len_hbm, q_hbm, k_hbm, v_hbm, out_hbm, lens, qv, kv, s_scr, stage, peak_scr, total_scr, acc_scr,
           local_sem, main_send, main_recv, aux_send, aux_recv, out_send, out_recv, ready):
    tokens, width = qv.shape
    heads = width // HEAD
    rows = tokens // n_kvh
    half = n_kvh // 2
    me = lax.axis_index("seq")
    mine = lax.axis_index("kvh")
    core = lax.rem(me, 2)
    my_hi = mine // half
    my_lo = lax.rem(mine, half)

    def seq_at(step):
        return lax.rem(me + (step + n_seq), n_seq)

    def peer(r):
        cross = r < half
        hi = jnp.where(cross, 1 - my_hi, my_hi)
        lo = lax.rem(my_lo + jnp.where(cross, r, r - half + 1), half)
        return hi * half + lo

    local = [
        pltpu.make_async_copy(k_hbm, kv.at[0, :tokens], local_sem.at[0]),
        pltpu.make_async_copy(v_hbm, kv.at[0, tokens:], local_sem.at[1]),
        pltpu.make_async_copy(q_hbm, qv, local_sem.at[2]),
        pltpu.make_async_copy(len_hbm, lens, local_sem.at[3]),
    ]
    for copy in local:
        copy.start()

    barrier = pltpu.get_barrier_semaphore()
    for step in (-2, -1, 1, 2):
        pl.semaphore_signal(barrier, inc=1, device_id={"seq": seq_at(step)}, device_id_type=MESH)
    for r in range(half, n_kvh - 1):
        pl.semaphore_signal(barrier, inc=1, device_id={"kvh": peer(r)}, device_id_type=MESH)

    @pl.when(my_hi == 0)
    def _():
        for r in range(half):
            pl.semaphore_signal(barrier, inc=1, device_id={"kvh": peer(r)}, device_id_type=MESH)

    local[0].wait()
    local[1].wait()
    pl.semaphore_wait(barrier, 4 + (half - 1) + my_hi * half)

    @pl.when(my_hi == 1)
    def _():
        for r in range(half):
            pl.semaphore_signal(ready, inc=1, device_id={"kvh": peer(r)}, device_id_type=MESH)


    piece = 2 * tokens // PARTS

    def main_copy(t, part):
        span = pl.ds(part * piece, piece)
        return pltpu.make_async_remote_copy(
            src_ref=kv.at[2 * t, span], dst_ref=kv.at[2 * t + 2, span],
            send_sem=main_send.at[t, part], recv_sem=main_recv.at[t, part],
            device_id={"seq": seq_at(2)}, device_id_type=MESH)

    def aux_copy(u, part, src, step):
        span = pl.ds(part * piece, piece)
        return pltpu.make_async_remote_copy(
            src_ref=kv.at[src, span], dst_ref=kv.at[2 * u + 1, span],
            send_sem=aux_send.at[u, part], recv_sem=aux_recv.at[u, part],
            device_id={"seq": seq_at(step)}, device_id_type=MESH)

    far = lax.rem(me // 2, RUN) >= RUN // 2
    first_r = jnp.where(far, half, 0)
    lead_row = pl.multiple_of(peer(first_r) * rows, rows)
    group = heads // PARTS

    def seen(b):
        return b * tokens <= base - first

    def lead(blocks, part):
        fresh = blocks[0] == 0
        where = pl.ds(part * group * rows, group * rows)
        q = jnp.concatenate(
            [qv[pl.ds(lead_row, rows), h * HEAD:(h + 1) * HEAD]
             for h in range(part * group, (part + 1) * group)], axis=0)
        scores = []
        for b in blocks:
            s = lax.dot_general(q, kv[b, :tokens], (((1,), (1,)), ((), ())),
                                preferred_element_type=jnp.float32)
            if b == 0:
                token = lead_row + lax.rem(lax.broadcasted_iota(jnp.int32, s.shape, 0), rows)
                s = jnp.where(lax.broadcasted_iota(jnp.int32, s.shape, 1) <= token, s, LOW)
            scores.append(s)
        old = jnp.full((group * rows, HEAD), LOW, jnp.float32) if fresh else peak_scr[where, :]
        best = old[:, :1]
        for b, s in zip(blocks, scores):
            top = jnp.max(s, axis=1, keepdims=True)
            best = jnp.maximum(best, top if b == 0 else jnp.where(seen(b), top, LOW))
        total = jnp.zeros((group * rows, HEAD), jnp.float32)
        acc = jnp.zeros((group * rows, HEAD), jnp.float32)
        for b, s in zip(blocks, scores):
            shift = best if b == 0 else jnp.where(seen(b), best, -LOW)
            p = jnp.exp2((s - shift) * EXP2_SCALE)
            for j in range(tokens // HEAD):
                total = total + p[:, j * HEAD:(j + 1) * HEAD]
            acc = acc + jnp.dot(p.astype(jnp.bfloat16), kv[b, tokens:], preferred_element_type=jnp.float32)
        if not fresh:
            shrink = jnp.exp2((old - best) * EXP2_SCALE)
            total = total + total_scr[where, :] * shrink
            acc = acc + acc_scr[where, :] * shrink
        peak_scr[where, :] = jnp.broadcast_to(best, (group * rows, HEAD))
        total_scr[where, :] = total
        acc_scr[where, :] = acc

    def aux_wait(u):
        for part in range(PARTS):
            aux_copy(u, part, 0, 1).wait_recv()

    for t in range(SPAN // 2):
        for part in range(PARTS):
            if t > 0:
                main_copy(t - 1, part).wait_recv()
            if t < SPAN // 2 - 1:
                main_copy(t, part).start()

            @pl.when(core == 0)
            def _():
                aux_copy(t, part, 2 * t, 1).start()

            if t > 0:
                @pl.when(core == 1)
                def _():
                    aux_copy(t - 1, part, 2 * t, -1).start()
            if t == SPAN // 2 - 1:
                @pl.when(core == 1)
                def _():
                    aux_copy(t, part, 2 * t, 1).start()
            if t > 0:
                if t > 1 and part == 0:
                    aux_wait(t - 2)
                lead((0,) if t == 1 else (2 * t - 2, 2 * t - 3), part)
        if t == 0:
            local[2].wait()
            local[3].wait()
            base = me * tokens
            first = jnp.int32(0)
            start = jnp.int32(0)
            for a in range(lens.shape[0]):
                first = jnp.where(start <= base, start, first)
                start = start + lens[a]

    for blocks in ((SPAN - 2, SPAN - 3), (SPAN - 1,)):
        aux_wait((blocks[-1] - 1) // 2)
        for part in range(PARTS):
            lead(blocks, part)

    def attend(row0):
        q = jnp.concatenate(
            [qv[pl.ds(row0, rows), h * HEAD:(h + 1) * HEAD] for h in range(heads)], axis=0)
        peak = jnp.full((heads * rows, HEAD), LOW, jnp.float32)
        for b in range(SPAN):
            s = lax.dot_general(q, kv[b, :tokens], (((1,), (1,)), ((), ())),
                                preferred_element_type=jnp.float32)
            if b == 0:
                token = row0 + lax.rem(lax.broadcasted_iota(jnp.int32, s.shape, 0), rows)
                s = jnp.where(lax.broadcasted_iota(jnp.int32, s.shape, 1) <= token, s, LOW)
            s_scr[:, b * tokens:(b + 1) * tokens] = s
            best = s[:, :HEAD]
            for j in range(1, tokens // HEAD):
                best = jnp.maximum(best, s[:, j * HEAD:(j + 1) * HEAD])
            if b > 0:
                best = jnp.where(seen(b), best, LOW)
            peak = jnp.maximum(peak, best)
        peak = jnp.max(peak, axis=1, keepdims=True)
        total = jnp.zeros((heads * rows, HEAD), jnp.float32)
        acc = jnp.zeros((heads * rows, HEAD), jnp.float32)
        for b in range(SPAN):
            shift = peak if b == 0 else jnp.where(seen(b), peak, -LOW)
            p = jnp.exp2((s_scr[:, b * tokens:(b + 1) * tokens] - shift) * EXP2_SCALE)
            for j in range(tokens // HEAD):
                total = total + p[:, j * HEAD:(j + 1) * HEAD]
            acc = acc + jnp.dot(p.astype(jnp.bfloat16), kv[b, tokens:], preferred_element_type=jnp.float32)
        return (acc / jnp.sum(total, axis=1, keepdims=True)).astype(jnp.bfloat16)

    columns = pl.ds(pl.multiple_of(mine * width, width), width)

    def out_copy(r):
        return pltpu.make_async_remote_copy(
            src_ref=stage.at[r], dst_ref=out_hbm.at[:, columns],
            send_sem=out_send.at[r], recv_sem=out_recv.at[r],
            device_id={"kvh": peer(r)}, device_id_type=MESH)

    def finish(r, done):
        for h in range(heads):
            stage[r, :, h * HEAD:(h + 1) * HEAD] = done[h * rows:(h + 1) * rows, :]

        @pl.when(r < n_kvh - 1)
        def _():
            out_copy(r).start()

    @pl.when(my_hi == 0)
    def _():
        pl.semaphore_wait(ready, half)

    finish(first_r, (acc_scr[...] / jnp.sum(total_scr[...], axis=1, keepdims=True)).astype(jnp.bfloat16))

    def one_chunk(i, carry):
        r = lax.rem(i + first_r, n_kvh)
        target = jnp.where(r == n_kvh - 1, mine, peer(r))
        finish(r, attend(pl.multiple_of(target * rows, rows)))
        return carry

    lax.fori_loop(1, n_kvh, one_chunk, 0)
    self_copy = pltpu.make_async_copy(stage.at[n_kvh - 1], out_hbm.at[:, columns], local_sem.at[0])
    self_copy.start()
    self_copy.wait()
    for r in range(n_kvh - 1):
        out_copy(r).wait()
    for t in range(SPAN // 2):
        for part in range(PARTS):
            if t < SPAN // 2 - 1:
                main_copy(t, part).wait_send()
            aux_copy(t, part, 0, 1).wait_send()


def shards(queries, keys, values, answer_lengths):
    tokens, width = queries.shape
    n_seq, n_kvh = lax.axis_size("seq"), lax.axis_size("kvh")
    rows = tokens // n_kvh
    heads = width // HEAD
    dma = pltpu.SemaphoreType.DMA
    hbm_spec = pl.BlockSpec(memory_space=pltpu.HBM)
    return pl.pallas_call(
        functools.partial(kernel, n_seq, n_kvh),
        out_shape=jax.ShapeDtypeStruct((rows, n_kvh * width), jnp.bfloat16),
        in_specs=[hbm_spec] * 4,
        out_specs=pl.BlockSpec(memory_space=pl.ANY),
        scratch_shapes=[
            pltpu.SMEM(answer_lengths.shape, jnp.int32),
            pltpu.VMEM((tokens, width), jnp.bfloat16),
            pltpu.VMEM((SPAN, 2 * tokens, HEAD), jnp.bfloat16),
            pltpu.VMEM((heads * rows, SPAN * tokens), jnp.float32),
            pltpu.VMEM((n_kvh, rows, width), jnp.bfloat16),
            pltpu.VMEM((heads * rows, HEAD), jnp.float32),
            pltpu.VMEM((heads * rows, HEAD), jnp.float32),
            pltpu.VMEM((heads * rows, HEAD), jnp.float32),
            dma((4,)),
            dma((SPAN // 2, PARTS)),
            dma((SPAN // 2, PARTS)),
            dma((SPAN // 2, PARTS)),
            dma((SPAN // 2, PARTS)),
            dma((n_kvh,)),
            dma((n_kvh,)),
            pltpu.SemaphoreType.REGULAR,
        ],
        compiler_params=pltpu.CompilerParams(
            collective_id=0, has_side_effects=True, vmem_limit_bytes=63 * 1024 * 1024),
        cost_estimate=pl.CostEstimate(
            flops=4 * tokens * width * SPAN * tokens,
            bytes_accessed=4 * tokens * width,
            transcendentals=tokens * heads * SPAN * tokens),
    )(answer_lengths, queries, keys, values)


def solution(mesh):
    in_specs = (P("seq", "kvh"), P("seq", "kvh"), P("seq", "kvh"), P())
    out_specs = P(("seq", "kvh"), None)
    return jax.shard_map(shards, mesh=mesh, in_specs=in_specs, out_specs=out_specs, check_vma=False)
```

time: 86.5 us -> 81.2 us (0.939)
  the two profiles are of different devices: /device:TPU:153 before, /device:TPU:193 now
where the time goes in v1:
time: 81.2 us; the launch traced here: 81 us
  Pallas kernels  78.9 us (97%)
  local copies, waits for them, and re-layouts  2.06 us (3%)
    pallas_call x1, Pallas kernels, shards(): pl.pallas_call(functools.partial(kernel, n_seq, n_kvh), out_shape=jax.Sha...  78.9 us
    unnamed x1, local copies, waits for them, and re-layouts  2.06 us

profile of v1, /device:TPU:193, one launch (start us, length us, event | category | flops | bytes accessed | tf_op | source)
XLA Modules:
  0.0 81.0 jit_solution(11323466793508051161)
XLA Ops:
  0.0 78.9 %shard_map.46 = bf16[32,12288]{1,0:T(8,128)(2,1)} custom-call(s32[16]{0:T(128)} %len_hbm.1, bf16[256,1536]{1,0:T(8,128)(2,1)} %q_hbm.1, bf16[256,128]{1,0:T(8,128)(2,1)} %k_hbm.1, bf16[256,128]{1,0:T(8,128)(2,1)} %v_hbm.1), custom_call_target="tpu_custom_call" | custom-call | flops 4831838208 | bytes 1572864 | tf_op jit(solution)/shard_map/pallas_call | solution.py:248
  79.0 2.1 %copy.6 = bf16[32,12288]{1,0:T(8,128)(2,1)} copy(bf16[32,12288]{1,0:T(8,128)(2,1)} %shard_map.46) | data formatting | bytes 1572864

commit v2 on v1

--- a/solution.py
+++ b/solution.py
@@ -12,13 +12,14 @@
 SPAN = 12
 PARTS = 4
 RUN = 8
+FAR_STEP = (0, 1, 1, 2, 2)
 MESH = pl.DeviceIdType.MESH
 LOW = -1e30
 EXP2_SCALE = math.log2(math.e) / math.sqrt(HEAD)
 
 
 def kernel(n_seq, n_kvh, len_hbm, q_hbm, k_hbm, v_hbm, out_hbm, lens, qv, kv, s_scr, stage, peak_scr, total_scr, acc_scr,
-           local_sem, main_send, main_recv, aux_send, aux_recv, out_send, out_recv, ready):
+           local_sem, main_send, main_recv, aux_send, aux_recv, far_send, out_send, out_recv, ready):
     tokens, width = qv.shape
     heads = width // HEAD
     rows = tokens // n_kvh
@@ -26,6 +27,8 @@
     me = lax.axis_index("seq")
     mine = lax.axis_index("kvh")
     core = lax.rem(me, 2)
+    chip = lax.rem(me // 2, RUN)
+    last = SPAN // 2 - 1
     my_hi = mine // half
     my_lo = lax.rem(mine, half)
 
@@ -48,8 +51,20 @@
         copy.start()
 
     barrier = pltpu.get_barrier_semaphore()
-    for step in (-2, -1, 1, 2):
-        pl.semaphore_signal(barrier, inc=1, device_id={"seq": seq_at(step)}, device_id_type=MESH)
+    greets = [(-2, core >= 0), (1 - 2 * core, core >= 0), (-1, (core == 0) & (chip > 0))]
+    greets += [(-2 * m, chip == 0) for m in range(2, last + 1)]
+    greets += [(-2 * last - 1, (core == 0) & (chip == 0))]
+    for step, known in greets:
+        @pl.when(known)
+        def _():
+            pl.semaphore_signal(barrier, inc=1, device_id={"seq": seq_at(step)}, device_id_type=MESH)
+    tail = (core == 1) & (chip < RUN - 1)
+    far_even = (chip >= RUN - last) & (chip < RUN - 1)
+    far_odd = (core == 1) & (chip == RUN - last - 1)
+    greeted = half - 1 + my_hi * half + 2
+    for known in (tail, far_even, far_odd):
+        greeted = greeted + known.astype(jnp.int32)
+
     for r in range(half, n_kvh - 1):
         pl.semaphore_signal(barrier, inc=1, device_id={"kvh": peer(r)}, device_id_type=MESH)
 
@@ -60,7 +75,7 @@
 
     local[0].wait()
     local[1].wait()
-    pl.semaphore_wait(barrier, 4 + (half - 1) + my_hi * half)
+    pl.semaphore_wait(barrier, greeted)
 
     @pl.when(my_hi == 1)
     def _():
@@ -77,15 +92,32 @@
             send_sem=main_send.at[t, part], recv_sem=main_recv.at[t, part],
             device_id={"seq": seq_at(2)}, device_id_type=MESH)
 
-    def aux_copy(u, part, src, step):
+    def aux_copy(u, src, step):
+        return pltpu.make_async_remote_copy(
+            src_ref=kv.at[src], dst_ref=kv.at[2 * u + 1],
+            send_sem=aux_send.at[u], recv_sem=aux_recv.at[u],
+            device_id={"seq": seq_at(step)}, device_id_type=MESH)
+
+    def far_copy(part):
         span = pl.ds(part * piece, piece)
-        return pltpu.make_async_remote_copy(
-            src_ref=kv.at[src, span], dst_ref=kv.at[2 * u + 1, span],
-            send_sem=aux_send.at[u, part], recv_sem=aux_recv.at[u, part],
-            device_id={"seq": seq_at(step)}, device_id_type=MESH)
-
-    far = lax.rem(me // 2, RUN) >= RUN // 2
-    first_r = jnp.where(far, half, 0)
+        m = RUN - chip
+        return pltpu.make_async_remote_copy(
+            src_ref=kv.at[0, span], dst_ref=kv.at[2 * m, span],
+            send_sem=far_send.at[0, part], recv_sem=main_recv.at[m - 1, part],
+            device_id={"seq": seq_at(2 * m)}, device_id_type=MESH)
+
+    def far_odd_copy():
+        return pltpu.make_async_remote_copy(
+            src_ref=kv.at[0], dst_ref=kv.at[2 * last + 1],
+            send_sem=far_send.at[1, 0], recv_sem=aux_recv.at[last],
+            device_id={"seq": seq_at(2 * last + 1)}, device_id_type=MESH)
+
+    hold = jnp.where((my_hi == 0) & (chip < last), half, 0)
+
+    def chunk(i):
+        return jnp.where(i < hold, half + i, jnp.where(i < hold + half, i - hold, i))
+
+    first_r = chunk(0)
     lead_row = pl.multiple_of(peer(first_r) * rows, rows)
     group = heads // PARTS
 
@@ -128,28 +160,38 @@
         acc_scr[where, :] = acc
 
     def aux_wait(u):
-        for part in range(PARTS):
-            aux_copy(u, part, 0, 1).wait_recv()
-
-    for t in range(SPAN // 2):
+        aux_copy(u, 0, 1).wait_recv()
+
+    for t in range(last + 1):
         for part in range(PARTS):
             if t > 0:
                 main_copy(t - 1, part).wait_recv()
-            if t < SPAN // 2 - 1:
+            if t == 0:
                 main_copy(t, part).start()
-
-            @pl.when(core == 0)
-            def _():
-                aux_copy(t, part, 2 * t, 1).start()
-
-            if t > 0:
-                @pl.when(core == 1)
+            elif t < last:
+                @pl.when(chip < RUN - 1)
                 def _():
-                    aux_copy(t - 1, part, 2 * t, -1).start()
-            if t == SPAN // 2 - 1:
-                @pl.when(core == 1)
-                def _():
-                    aux_copy(t, part, 2 * t, 1).start()
+                    main_copy(t, part).start()
+            for m in range(2, last + 1):
+                if t == FAR_STEP[m - 2]:
+                    @pl.when(chip == RUN - m)
+                    def _():
+                        far_copy(part).start()
+            if part == PARTS - 1:
+                if t == 0:
+                    @pl.when(core == 0)
+                    def _():
+                        aux_copy(0, 0, 1).start()
+                else:
+                    aux_copy(t - core, 2 * t, 1 - 2 * core).start()
+                if t == last:
+                    @pl.when(tail)
+                    def _():
+                        aux_copy(last, 2 * last, 1).start()
+                if t == FAR_STEP[-1]:
+                    @pl.when(far_odd)
+                    def _():
+                        far_odd_copy().start()
             if t > 0:
                 if t > 1 and part == 0:
                     aux_wait(t - 2)
@@ -220,7 +262,7 @@
     finish(first_r, (acc_scr[...] / jnp.sum(total_scr[...], axis=1, keepdims=True)).astype(jnp.bfloat16))
 
     def one_chunk(i, carry):
-        r = lax.rem(i + first_r, n_kvh)
+        r = chunk(i)
         target = jnp.where(r == n_kvh - 1, mine, peer(r))
         finish(r, attend(pl.multiple_of(target * rows, rows)))
         return carry
@@ -231,11 +273,28 @@
     self_copy.wait()
     for r in range(n_kvh - 1):
         out_copy(r).wait()
-    for t in range(SPAN // 2):
-        for part in range(PARTS):
-            if t < SPAN // 2 - 1:
+    for part in range(PARTS):
+        main_copy(0, part).wait_send()
+
+        @pl.when(chip < RUN - 1)
+        def _():
+            for t in range(1, last):
                 main_copy(t, part).wait_send()
-            aux_copy(t, part, 0, 1).wait_send()
+
+        @pl.when(far_even)
+        def _():
+            far_copy(part).wait_send()
+
+    for u in range(last):
+        aux_copy(u, 0, 1).wait_send()
+
+    @pl.when((core == 0) | tail)
+    def _():
+        aux_copy(last, 0, 1).wait_send()
+
+    @pl.when(far_odd)
+    def _():
+        far_odd_copy().wait_send()
 
 
 def shards(queries, keys, values, answer_lengths):
@@ -262,8 +321,9 @@
             dma((4,)),
             dma((SPAN // 2, PARTS)),
             dma((SPAN // 2, PARTS)),
-            dma((SPAN // 2, PARTS)),
-            dma((SPAN // 2, PARTS)),
+            dma((SPAN // 2,)),
+            dma((SPAN // 2,)),
+            dma((2, PARTS)),
             dma((n_kvh,)),
             dma((n_kvh,)),
             pltpu.SemaphoreType.REGULAR,

time: 81.2 us -> 79.2 us (0.975)
  the two profiles are of different devices: /device:TPU:193 before, /device:TPU:91 now
where the time goes in v2:
time: 79.2 us; the launch traced here: 79 us
  Pallas kernels  76.9 us (97%)
  local copies, waits for them, and re-layouts  2.06 us (3%)
    pallas_call x1, Pallas kernels, shards(): pl.pallas_call(functools.partial(kernel, n_seq, n_kvh), out_shape=jax.Sha...  76.9 us
    unnamed x1, local copies, waits for them, and re-layouts  2.06 us

profile of v2, /device:TPU:91, one launch (start us, length us, event | category | flops | bytes accessed | tf_op | source)
XLA Modules:
  0.0 79.0 jit_solution(11368436223754836649)
XLA Ops:
  0.0 76.9 %shard_map.46 = bf16[32,12288]{1,0:T(8,128)(2,1)} custom-call(s32[16]{0:T(128)} %len_hbm.1, bf16[256,1536]{1,0:T(8,128)(2,1)} %q_hbm.1, bf16[256,128]{1,0:T(8,128)(2,1)} %k_hbm.1, bf16[256,128]{1,0:T(8,128)(2,1)} %v_hbm.1), custom_call_target="tpu_custom_call" | custom-call | flops 4831838208 | bytes 1572864 | tf_op jit(solution)/shard_map/pallas_call | solution.py:307
  76.9 2.1 %copy.6 = bf16[32,12288]{1,0:T(8,128)(2,1)} copy(bf16[32,12288]{1,0:T(8,128)(2,1)} %shard_map.46) | data formatting | bytes 1572864

commit v3 on v2

--- a/solution.py
+++ b/solution.py
@@ -12,7 +12,7 @@
 SPAN = 12
 PARTS = 4
 RUN = 8
-FAR_STEP = (0, 1, 1, 2, 2)
+FAR_STEP = (0, 0, 0, 0, 0)
 MESH = pl.DeviceIdType.MESH
 LOW = -1e30
 EXP2_SCALE = math.log2(math.e) / math.sqrt(HEAD)
@@ -112,7 +112,7 @@
             send_sem=far_send.at[1, 0], recv_sem=aux_recv.at[last],
             device_id={"seq": seq_at(2 * last + 1)}, device_id_type=MESH)
 
-    hold = jnp.where((my_hi == 0) & (chip < last), half, 0)
+    hold = jnp.where(my_hi == 0, half, 0)
 
     def chunk(i):
         return jnp.where(i < hold, half + i, jnp.where(i < hold + half, i - hold, i))
@@ -211,17 +211,18 @@
         for part in range(PARTS):
             lead(blocks, part)
 
-    def attend(row0):
+    def attend_heads(row0, part):
+        where = pl.ds(part * group * rows, group * rows)
         q = jnp.concatenate(
-            [qv[pl.ds(row0, rows), h * HEAD:(h + 1) * HEAD] for h in range(heads)], axis=0)
-        peak = jnp.full((heads * rows, HEAD), LOW, jnp.float32)
+            [qv[pl.ds(row0, rows), h * HEAD:(h + 1) * HEAD] for h in range(part * group, (part + 1) * group)], axis=0)
+        peak = jnp.full((group * rows, HEAD), LOW, jnp.float32)
         for b in range(SPAN):
             s = lax.dot_general(q, kv[b, :tokens], (((1,), (1,)), ((), ())),
                                 preferred_element_type=jnp.float32)
             if b == 0:
                 token = row0 + lax.rem(lax.broadcasted_iota(jnp.int32, s.shape, 0), rows)
                 s = jnp.where(lax.broadcasted_iota(jnp.int32, s.shape, 1) <= token, s, LOW)
-            s_scr[:, b * tokens:(b + 1) * tokens] = s
+            s_scr[where, b * tokens:(b + 1) * tokens] = s
             best = s[:, :HEAD]
             for j in range(1, tokens // HEAD):
                 best = jnp.maximum(best, s[:, j * HEAD:(j + 1) * HEAD])
@@ -229,15 +230,18 @@
                 best = jnp.where(seen(b), best, LOW)
             peak = jnp.maximum(peak, best)
         peak = jnp.max(peak, axis=1, keepdims=True)
-        total = jnp.zeros((heads * rows, HEAD), jnp.float32)
-        acc = jnp.zeros((heads * rows, HEAD), jnp.float32)
+        total = jnp.zeros((group * rows, HEAD), jnp.float32)
+        acc = jnp.zeros((group * rows, HEAD), jnp.float32)
         for b in range(SPAN):
             shift = peak if b == 0 else jnp.where(seen(b), peak, -LOW)
-            p = jnp.exp2((s_scr[:, b * tokens:(b + 1) * tokens] - shift) * EXP2_SCALE)
+            p = jnp.exp2((s_scr[where, b * tokens:(b + 1) * tokens] - shift) * EXP2_SCALE)
             for j in range(tokens // HEAD):
                 total = total + p[:, j * HEAD:(j + 1) * HEAD]
             acc = acc + jnp.dot(p.astype(jnp.bfloat16), kv[b, tokens:], preferred_element_type=jnp.float32)
         return (acc / jnp.sum(total, axis=1, keepdims=True)).astype(jnp.bfloat16)
+
+    def attend(row0):
+        return jnp.concatenate([attend_heads(row0, part) for part in range(PARTS)], axis=0)
 
     columns = pl.ds(pl.multiple_of(mine * width, width), width)
 

time: 79.2 us -> 79.4 us (level)
  the two profiles are of different devices: /device:TPU:91 before, /device:TPU:40 now
where the time goes in v3:
time: 79.4 us; the launch traced here: 79.2 us
  Pallas kernels  77.2 us (97%)
  local copies, waits for them, and re-layouts  2.06 us (3%)
    pallas_call x1, Pallas kernels, shards(): pl.pallas_call(functools.partial(kernel, n_seq, n_kvh), out_shape=jax.Sha...  77.2 us
    unnamed x1, local copies, waits for them, and re-layouts  2.06 us

profile of v3, /device:TPU:40, one launch (start us, length us, event | category | flops | bytes accessed | tf_op | source)
XLA Modules:
  0.0 79.2 jit_solution(6248347798471364925)
XLA Ops:
  0.0 77.2 %shard_map.46 = bf16[32,12288]{1,0:T(8,128)(2,1)} custom-call(s32[16]{0:T(128)} %len_hbm.1, bf16[256,1536]{1,0:T(8,128)(2,1)} %q_hbm.1, bf16[256,128]{1,0:T(8,128)(2,1)} %k_hbm.1, bf16[256,128]{1,0:T(8,128)(2,1)} %v_hbm.1), custom_call_target="tpu_custom_call" | custom-call | flops 4831838208 | bytes 1572864 | tf_op jit(solution)/shard_map/pallas_call | solution.py:311
  77.2 2.1 %copy.6 = bf16[32,12288]{1,0:T(8,128)(2,1)} copy(bf16[32,12288]{1,0:T(8,128)(2,1)} %shard_map.46) | data formatting | bytes 1572864
